TPU v7x, 512 devices: a whole 4x4x16 slice. The times are simulated.
512 devices in a mesh: areal: 32 (over y, x, core), layer: 16 (over z).
Axes of the slice: x: 4, y: 4, z: 16, core: 2. Of those that a mesh axis runs over, the one named last changes fastest.
Arguments:
- rhs: bfloat16 [32, 32, 112, 384], P('areal', 'layer'), may hold values from -6 to 6
- areal_blocks: bfloat16 [32, 32, 6, 384, 384], P('areal', 'layer'), may hold values from -0.078125 to 0.078125
- vertical_blocks: bfloat16 [32, 32, 2, 384, 384], P('areal', 'layer'), may hold values from -0.078125 to 0.078125
- conn_src: int32 [32, 16, 6], P('areal', 'layer'), may hold values from 0 to 63, as said below
- conn_count: int32 [32, 16], P('areal', 'layer'), may hold values from 1 to 6, as said below
- tile_map: int32 [64], replicated, may hold values from 0 to 63, as said below
- well_cells: int32 [32, 32, 4], P('areal', 'layer'), may hold values from 0 to 127
- well_gain: float32 [32, 32, 4], P('areal', 'layer'), may hold values from -24 to 24
- sens: float32 [32, 32, 3, 128], P('areal', 'layer'), may hold values from -6 to 6
- basis: bfloat16 [32, 32, 128, 256], P('areal', 'layer'), may hold values from -0.015625 to 0.015625
Outputs:
- adjoint: bfloat16 [32, 32, 112, 384], P('areal', 'layer')
- coefficients: bfloat16 [112, 256], P('layer', 'areal')
Inputs may be any that keep to these rules, and one draw needn't show every extreme that they name: Tile t of a layer group's plane is held by device column tile_map[t] // 2 in tile layer 2 g + tile_map[t] % 2; each value is held by one tile. `conn_src`: the 6 sources of device column c lie, in some order, on the 6 device columns (c + k) mod 32 with k one of 1 to 2, their negatives, 16 and 17, one on each. `conn_count`: the live connections of a device are its first ones. `well_cells`: cells of a tile, repeats allowed.
All inputs are finite; a program needn't handle non-finite values.
Results may differ from a plain program's by a relative error of at most 0.02.
Values may be sent and summed in bfloat16 or wider, within the bound.
A program may use at most 64 MiB of HBM per device.

v0:
```python
import jax
import jax.numpy as jnp
from jax import lax
from jax.sharding import PartitionSpec as P

ITERS = 3


def extended(x, sides, width):
    for axis, dim in sides:
        size, length = (lax.axis_size(axis), x.shape[dim])
        up = [(i, (i + 1) % size) for i in range(size - 1)]
        down = [(j, i) for i, j in up]
        last = lax.slice_in_dim(x, length - width, length, axis=dim)
        leading = lax.slice_in_dim(x, 0, width, axis=dim)
        before = lax.ppermute(last, axis, up)
        after = lax.ppermute(leading, axis, down)
        x = jnp.concatenate([before, x, after], axis=dim)
    return x


def on_device(
    rhs,
    areal_blocks,
    vertical_blocks,
    conn_src,
    conn_count,
    tile_map,
    well_cells,
    well_gain,
    sens,
    basis,
):
    cells = sens.shape[-1]
    phases = sens.shape[-2]
    rows = rhs.shape[2]
    sources = conn_src[0, 0]
    place = jnp.take(tile_map, sources)
    peer = place // 2
    slot = place % 2
    live = jnp.arange(sources.shape[0], dtype=jnp.int32) < conn_count[0, 0]
    blocks = areal_blocks[0]
    vert_blocks = vertical_blocks[0]
    rhs_float = rhs[0].astype(jnp.float32)
    lam = rhs
    for step in range(ITERS):
        whole = lax.all_gather(lam, "areal", axis=0, tiled=True)
        chosen = whole[peer, slot]
        chosen = jnp.where(live[:, None, None], chosen, jnp.zeros_like(chosen))
        padded = extended(lam, (("layer", 1),), 1)[0]
        near = jnp.stack([padded[0:2], padded[2:4]], axis=1)
        off = jnp.einsum("sru,dsuv->drv", chosen, blocks, preferred_element_type=jnp.float32)
        off = off + jnp.einsum(
            "dkru,dkuv->drv", near, vert_blocks, preferred_element_type=jnp.float32
        )
        lam = (rhs_float - off).astype(jnp.bfloat16)[None]
    lamf = lam[0].astype(jnp.float32).reshape(2, rows, phases, cells)
    grad = jnp.sum(lamf * sens[0][:, None, :, :], axis=2)
    hits = well_cells[0][:, :, None] == jnp.arange(cells, dtype=jnp.int32)[None, None, :]
    well_sum = jnp.sum(jnp.where(hits, well_gain[0][:, :, None], 0.0), axis=1)
    grad = (grad + well_sum[:, None, :] * lamf[:, :, 0, :]).astype(jnp.bfloat16)
    partial_sum = jnp.einsum("jrc,jcm->rm", grad, basis[0], preferred_element_type=jnp.float32)
    reduced = lax.psum_scatter(partial_sum, "areal", scatter_dimension=1, tiled=True)
    reduced = lax.psum_scatter(reduced, "layer", scatter_dimension=0, tiled=True)
    return (lam, reduced.astype(jnp.bfloat16))


def solution(mesh):
    in_specs = (
        P("areal", "layer", None, None),
        P("areal", "layer", None, None, None),
        P("areal", "layer", None, None, None),
        P("areal", "layer", None),
        P("areal", "layer"),
        P(),
        P("areal", "layer", None),
        P("areal", "layer", None),
        P("areal", "layer", None, None),
        P("areal", "layer", None, None),
    )
    out_specs = (P("areal", "layer", None, None), P("layer", "areal"))
    return jax.shard_map(
        on_device, mesh=mesh, in_specs=in_specs, out_specs=out_specs, check_vma=False
    )
```

profile of v0, /device:TPU:6, one launch (start us, length us, event | category | flops | bytes accessed | tf_op | source)
XLA Modules:
  0.0 398.7 jit_solution(2308188141515170945)
XLA Ops:
  8.0 1.9 fusion.93
  9.9 4.4 %collective-permute-start = (bf16[1,1,112,384]{3,2,1,0:T(8,128)(2,1)}, bf16[1,1,112,384]{3,2,1,0:T(8,128)(2,1)}, u32[]{:S(2)}, u32[]{:S(2)}) collective-permute-start(bf16[1,1,112,384]{3,2,1,0:T(8,128)(2,1)} %get-tuple-element.20), channel_id=1, source_target_pairs={{0,1},{1,2},{2,3},{3,4},{4,5},{5,6},{6,7},{7,8},{8,9},{9,10},{10,1... | collective-permute-start | bytes 258056 | tf_op jit(solution)/shard_map/ppermute | solution.py:16
  14.3 1.3 collective-permute-start.1
  16.9 1.3 gather_fusion
  18.9 2.1 collective-permute-done.1
  21.0 1.1 fusion.70
  22.0 2.4 convolution_bitcast_fusion.2
  24.4 53.8 %all-gather.6.cloned.1.call-done = bf16[32,2,112,384]{3,2,1,0:T(8,128)(2,1)} async-done(((bf16[1,2,112,384]{3,2,1,0:T(8,128)(2,1)}), bf16[32,2,112,384]{3,2,1,0:T(8,128)(2,1)}) %all-gather.6.cloned.1.call-update) | async-done | bytes 5505040 | tf_op jit(solution)/shard_map/all_gather | solution.py:47
  78.2 4.0 %gather_fusion.1 = bf16[6,112,384]{2,1,0:T(8,128)(2,1)} fusion(bf16[32,2,112,384]{3,2,1,0:T(8,128)(2,1)} %all-gather.6.cloned.1.call-done, s32[6]{0:T(128)S(1)} %fusion.82), kind=kCustom, calls=%fused_computation.1 | custom fusion | bytes 1032240 | tf_op jit(solution)/shard_map/gather | solution.py:48
  82.3 2.5 fusion.33
  85.8 3.5 collective-permute-start.2
  89.3 1.3 collective-permute-start.3
  91.5 4.2 %collective-permute-done.3 = bf16[1,1,112,384]{3,2,1,0:T(8,128)(2,1)S(1)} collective-permute-done((bf16[1,1,112,384]{3,2,1,0:T(8,128)(2,1)S(1)}, bf16[1,1,112,384]{3,2,1,0:T(8,128)(2,1)S(1)}, u32[]{:S(2)}, u32[]{:S(2)}) %collective-permute-start.3) | collective-permute-done | bytes 86048 | tf_op jit(solution)/shard_map/ppermute | solution.py:17
  95.7 1.0 fusion.68
  96.7 2.4 convolution_bitcast_fusion.1
  99.0 48.5 %all-gather.8.cloned.1.call-done = bf16[64,112,384]{2,1,0:T(8,128)(2,1)} async-done(((bf16[2,112,384]{2,1,0:T(8,128)(2,1)}), bf16[64,112,384]{2,1,0:T(8,128)(2,1)}) %all-gather.8.cloned.1.call-update) | async-done | bytes 5505040 | tf_op jit(solution)/shard_map/all_gather | solution.py:47
  147.5 4.0 %gather_fusion.2 = bf16[6,112,384]{2,1,0:T(8,128)(2,1)} fusion(bf16[32,2,112,384]{3,2,1,0:T(8,128)(2,1)} %bitcast.157, s32[6]{0:T(128)S(1)} %fusion.82), kind=kCustom, calls=%fused_computation.2 | custom fusion | bytes 1032240 | tf_op jit(solution)/shard_map/gather | solution.py:48
  151.5 2.5 fusion.36
  155.1 3.5 collective-permute-start.4
  158.6 1.3 collective-permute-start.5
  160.7 4.2 %collective-permute-done.5 = bf16[1,1,112,384]{3,2,1,0:T(8,128)(2,1)S(1)} collective-permute-done((bf16[1,1,112,384]{3,2,1,0:T(8,128)(2,1)S(1)}, bf16[1,1,112,384]{3,2,1,0:T(8,128)(2,1)S(1)}, u32[]{:S(2)}, u32[]{:S(2)}) %collective-permute-start.5) | collective-permute-done | bytes 86048 | tf_op jit(solution)/shard_map/ppermute | solution.py:17
  165.9 2.4 convolution_bitcast_fusion
  168.3 48.5 %all-gather.10.cloned.1.call-done = bf16[64,112,384]{2,1,0:T(8,128)(2,1)} async-done(((bf16[2,112,384]{2,1,0:T(8,128)(2,1)}), bf16[64,112,384]{2,1,0:T(8,128)(2,1)}) %all-gather.10.cloned.1.call-update) | async-done | bytes 5505040 | tf_op jit(solution)/shard_map/all_gather | solution.py:47
  216.8 4.0 %gather_fusion.3 = bf16[6,112,384]{2,1,0:T(8,128)(2,1)} fusion(bf16[32,2,112,384]{3,2,1,0:T(8,128)(2,1)} %bitcast.156, s32[6]{0:T(128)S(1)} %fusion.82), kind=kCustom, calls=%fused_computation.3 | custom fusion | bytes 1032240 | tf_op jit(solution)/shard_map/gather | solution.py:48
  220.8 2.5 fusion.39
  223.3 1.8 copy.34
  225.1 1.2 multiply_reduce_fusion
  226.3 1.9 convolution_bitcast_fusion.3
  228.2 1.3 dynamic-slice.2
  229.5 1.3 dynamic-slice
  232.1 127.4 %all-reduce.4.cloned.1.call-done = f32[112,256]{0,1:T(8,128)} async-done(((f32[112,256]{0,1:T(8,128)}), f32[112,256]{0,1:T(8,128)}) %all-reduce.4.cloned.1.call-update) | async-done | bytes 114704
  360.2 31.3 %all-reduce.1 = bf16[112,8]{0,1:T(8,128)(2,1)S(1)} all-reduce(f32[112,8]{0,1:T(8,128)S(1)} %constant_dynamic-slice_fusion), channel_id=5, replica_groups=mesh['areal'=32,'layer'=16] {'layer'}, use_global_device_ids=true, to_apply=%region_3.4.clone | all-reduce | flops 896 | bytes 5376
  (27 shorter events, 8.3 us)
Async XLA Ops:
  7.2 75.1 %copy-start = (bf16[1,2,6,384,384]{4,3,2,1,0:T(8,128)(2,1)S(1)}, bf16[1,2,6,384,384]{4,3,2,1,0:T(8,128)(2,1)}, u32[]{:S(2)}) copy-start(bf16[1,2,6,384,384]{4,3,2,1,0:T(8,128)(2,1)} %param.11) | copy-start | bytes 10616836
  7.2 71.1 %all-gather.6.cloned.1.call-start = ((), (), s32[]{:S(2)}) async-start(), calls=%async_computation | async-start | bytes 5677056 | tf_op jit(solution)/shard_map/all_gather | solution.py:47
  7.9 139.6 %all-gather.8.cloned.1.call-start = ((), (), s32[]{:S(2)}) async-start(), calls=%async_computation.1 | async-start | bytes 5677056 | tf_op jit(solution)/shard_map/all_gather | solution.py:47
  9.9 9.0 %collective-permute-start = (bf16[1,1,112,384]{3,2,1,0:T(8,128)(2,1)}, bf16[1,1,112,384]{3,2,1,0:T(8,128)(2,1)}, u32[]{:S(2)}, u32[]{:S(2)}) collective-permute-start(bf16[1,1,112,384]{3,2,1,0:T(8,128)(2,1)} %get-tuple-element.20), channel_id=1, source_target_pairs={{0,1},{1,2},{2,3},{3,4},{4,5},{5,6},{6,7},{7,8},{8,9},{9,10},{10,1... | collective-permute-start | bytes 258056 | tf_op jit(solution)/shard_map/ppermute | solution.py:16
  14.3 6.7 %collective-permute-start.1 = (bf16[1,1,112,384]{3,2,1,0:T(8,128)(2,1)}, bf16[1,1,112,384]{3,2,1,0:T(8,128)(2,1)}, u32[]{:S(2)}, u32[]{:S(2)}) collective-permute-start(bf16[1,1,112,384]{3,2,1,0:T(8,128)(2,1)} %get-tuple-element.21), channel_id=1, source_target_pairs={{1,0},{2,1},{3,2},{4,3},{5,4},{6,5},{7,6},{8,7},{9,8},{10,9},{11,1... | collective-permute-start | bytes 258056 | tf_op jit(solution)/shard_map/ppermute | solution.py:17
  84.8 131.9 %all-gather.10.cloned.1.call-start = ((), (), s32[]{:S(2)}) async-start(), calls=%async_computation.2 | async-start | bytes 5677056 | tf_op jit(solution)/shard_map/all_gather | solution.py:47
  85.8 5.6 %collective-permute-start.2 = (bf16[1,1,112,384]{3,2,1,0:T(8,128)(2,1)S(1)}, bf16[1,1,112,384]{3,2,1,0:T(8,128)(2,1)S(1)}, u32[]{:S(2)}, u32[]{:S(2)}) collective-permute-start(bf16[1,1,112,384]{3,2,1,0:T(8,128)(2,1)S(1)} %get-tuple-element.16), channel_id=1, source_target_pairs={{0,1},{1,2},{2,3},{3,4},{4,5},{5,6},{6,7},{7,8},{8,9},{9,10},{10,1... | collective-permute-start | bytes 258056 | tf_op jit(solution)/shard_map/ppermute | solution.py:16
  89.3 6.4 %collective-permute-start.3 = (bf16[1,1,112,384]{3,2,1,0:T(8,128)(2,1)S(1)}, bf16[1,1,112,384]{3,2,1,0:T(8,128)(2,1)S(1)}, u32[]{:S(2)}, u32[]{:S(2)}) collective-permute-start(bf16[1,1,112,384]{3,2,1,0:T(8,128)(2,1)S(1)} %get-tuple-element.17), channel_id=1, source_target_pairs={{1,0},{2,1},{3,2},{4,3},{5,4},{6,5},{7,6},{8,7},{9,8},{10,9},{11,1... | collective-permute-start | bytes 258056 | tf_op jit(solution)/shard_map/ppermute | solution.py:17
  96.7 57.5 %copy-start.1 = (f32[1,2,3,128]{3,1,2,0:T(2,128)S(1)}, f32[1,2,3,128]{3,1,2,0:T(2,128)}, u32[]{:S(2)}) copy-start(f32[1,2,3,128]{3,1,2,0:T(2,128)} %param.18) | copy-start | bytes 9220
  154.1 205.4 %all-reduce.4.cloned.1.call-start = ((), (), s32[]{:S(2)}) async-start(), calls=%async_computation.3 | async-start | bytes 262144
  155.1 5.6 %collective-permute-start.4 = (bf16[1,1,112,384]{3,2,1,0:T(8,128)(2,1)S(1)}, bf16[1,1,112,384]{3,2,1,0:T(8,128)(2,1)S(1)}, u32[]{:S(2)}, u32[]{:S(2)}) collective-permute-start(bf16[1,1,112,384]{3,2,1,0:T(8,128)(2,1)S(1)} %get-tuple-element.12), channel_id=1, source_target_pairs={{0,1},{1,2},{2,3},{3,4},{4,5},{5,6},{6,7},{7,8},{8,9},{9,10},{10,1... | collective-permute-start | bytes 258056 | tf_op jit(solution)/shard_map/ppermute | solution.py:16
  158.6 6.4 %collective-permute-start.5 = (bf16[1,1,112,384]{3,2,1,0:T(8,128)(2,1)S(1)}, bf16[1,1,112,384]{3,2,1,0:T(8,128)(2,1)S(1)}, u32[]{:S(2)}, u32[]{:S(2)}) collective-permute-start(bf16[1,1,112,384]{3,2,1,0:T(8,128)(2,1)S(1)} %get-tuple-element.13), channel_id=1, source_target_pairs={{1,0},{2,1},{3,2},{4,3},{5,4},{6,5},{7,6},{8,7},{9,8},{10,9},{11,1... | collective-permute-start | bytes 258056 | tf_op jit(solution)/shard_map/ppermute | solution.py:17
Sparse Core Ops, SparseCore 0:
  11.1 67.0 all-gather.5
  84.9 62.5 all-gather.7
  154.2 62.5 all-gather.9
  228.3 131.1 all-reduce.3
where the time goes:
time: 400 us; the launch traced here: 399 us
  waiting for transfers between devices  290 us (72%)
  blocking collectives  31.3 us (8%)
  local copies, waits for them, and re-layouts  22.9 us (6%)
  matrix products  16.6 us (4%)
  between operations  15.8 us (4%)
  starting transfers between devices  15.4 us (4%)
  other arithmetic  6.32 us (2%)
    all_gather x3, waiting for transfers between devices, on_device(): whole = lax.all_gather(lam, 'areal', axis=0, tiled=True)  151 us
    unnamed x5, waiting for transfers between devices  128 us
    unnamed x1, blocking collectives  31.3 us
    gather x3, local copies, waits for them, and re-layouts, on_device(): chosen = whole[peer, slot]  12 us
    ppermute x3, starting transfers between devices, extended(): before = lax.ppermute(last, axis, up)  11.4 us
    ppermute x3, waiting for transfers between devices, extended(): after = lax.ppermute(leading, axis, down)  10.5 us
  transfers between devices with their start and end apart: 10, of which 9 were waited for; matrix products, arithmetic and copies ran while one was open for 5% of the time, Pallas kernels for 0%

commit v1 on v0

--- a/solution.py
+++ b/solution.py
@@ -44,7 +44,8 @@
     rhs_float = rhs[0].astype(jnp.float32)
     lam = rhs
     for step in range(ITERS):
-        whole = lax.all_gather(lam, "areal", axis=0, tiled=True)
+        sent = jnp.stack([lam] * lax.axis_size("areal"))
+        whole = jnp.concatenate(lax.all_to_all(sent, "areal", 0, 0), axis=0)
         chosen = whole[peer, slot]
         chosen = jnp.where(live[:, None, None], chosen, jnp.zeros_like(chosen))
         padded = extended(lam, (("layer", 1),), 1)[0]

time: 400 us -> 437 us (1.093)
  starting transfers between devices: 15.4 us -> 37.3 us
  local copies, waits for them, and re-layouts: 22.9 us -> 33.2 us
  waiting for transfers between devices: 290 us -> 298 us
    all_to_all x0 -> x3, waiting for transfers between devices: none -> 155 us  [on_device(): whole = jnp.concatenate(lax.all_to_all(sent, 'areal', 0, 0), axis=0)]
    all_gather x3 -> x0, waiting for transfers between devices: 151 us -> none  [on_device(): whole = lax.all_gather(lam, 'areal', axis=0, tiled=True)]
    all_to_all x0 -> x3, starting transfers between devices: none -> 28.9 us  [on_device(): whole = jnp.concatenate(lax.all_to_all(sent, 'areal', 0, 0), axis=0)]
    another operation x0 -> x3, local copies, waits for them, and re-layouts: none -> 9.83 us  [on_device(): sent = jnp.stack([lam] * lax.axis_size('areal'))]
    ppermute x3, starting transfers between devices: 11.4 us -> 4.51 us  [extended(): before = lax.ppermute(last, axis, up)]
    unnamed x5 -> x2, waiting for transfers between devices: 128 us -> 129 us
  transfers between devices with their start and end apart: 10 -> 10, of which waited for: 9 -> 9; matrix products, arithmetic and copies ran while one was open for 5% -> 4% of each run, Pallas kernels for 0% -> 0%
where the time goes in v1:
time: 437 us; the launch traced here: 436 us
  waiting for transfers between devices  298 us (68%)
  starting transfers between devices  37.3 us (9%)
  local copies, waits for them, and re-layouts  33.2 us (8%)
  blocking collectives  31.3 us (7%)
  between operations  16.2 us (4%)
  matrix products  15.3 us (4%)
  other arithmetic  5 us (1%)
    all_to_all x3, waiting for transfers between devices, on_device(): whole = jnp.concatenate(lax.all_to_all(sent, 'areal', 0, 0), axis=0)  155 us
    unnamed x2, waiting for transfers between devices  129 us
    unnamed x1, blocking collectives  31.3 us
    all_to_all x3, starting transfers between devices, on_device(): whole = jnp.concatenate(lax.all_to_all(sent, 'areal', 0, 0), axis=0)  28.9 us
    ppermute x3, waiting for transfers between devices, extended(): after = lax.ppermute(leading, axis, down)  12.3 us
    gather x3, local copies, waits for them, and re-layouts, on_device(): chosen = whole[peer, slot]  12 us
    another operation x3, local copies, waits for them, and re-layouts, on_device(): sent = jnp.stack([lam] * lax.axis_size('areal'))  9.83 us
  transfers between devices with their start and end apart: 10, of which 9 were waited for; matrix products, arithmetic and copies ran while one was open for 4% of the time, Pallas kernels for 0%

profile of v1, /device:TPU:6, one launch (start us, length us, event | category | flops | bytes accessed | tf_op | source)
XLA Modules:
  0.0 436.0 jit_solution(6290745087045806727)
XLA Ops:
  7.2 4.0 stack.24
  11.2 10.5 %all-to-all-start = ((bf16[32,1,2,112,384]{4,3,2,1,0:T(8,128)(2,1)}), bf16[32,1,2,112,384]{4,3,2,1,0:T(8,128)(2,1)}, u32[]{:S(2)}, u32[]{:S(2)}) async-start(bf16[32,1,2,112,384]{4,3,2,1,0:T(8,128)(2,1)} %stack.24), calls=%async_computation | async-start | bytes 11010048 | tf_op jit(solution)/shard_map/all_to_all | solution.py:48
  21.7 1.6 fusion.93
  23.3 1.9 collective-permute-start
  27.9 4.1 collective-permute-done.1
  33.0 2.4 convolution_bitcast_fusion.2
  35.4 50.7 %all-to-all-done = bf16[32,1,2,112,384]{4,3,2,1,0:T(8,128)(2,1)} async-done(((bf16[32,1,2,112,384]{4,3,2,1,0:T(8,128)(2,1)}), bf16[32,1,2,112,384]{4,3,2,1,0:T(8,128)(2,1)}, u32[]{:S(2)}, u32[]{:S(2)}) %all-to-all-start) | async-done | bytes 5505056 | tf_op jit(solution)/shard_map/all_to_all | solution.py:48
  86.1 4.0 gather_fusion.1
  90.2 1.9 fusion.33
  92.7 2.9 stack.28
  95.6 9.2 %all-to-all-start.1 = ((bf16[32,1,2,112,384]{4,3,2,1,0:T(8,128)(2,1)}), bf16[32,1,2,112,384]{4,3,2,1,0:T(8,128)(2,1)}, u32[]{:S(2)}, u32[]{:S(2)}) async-start(bf16[32,1,2,112,384]{4,3,2,1,0:T(8,128)(2,1)} %stack.28), calls=%async_computation.1 | async-start | bytes 11010048 | tf_op jit(solution)/shard_map/all_to_all | solution.py:48
  105.7 1.3 collective-permute-start.2
  107.0 1.3 collective-permute-start.3
  109.4 4.1 collective-permute-done.3
  114.5 2.4 convolution_bitcast_fusion.1
  116.9 52.4 %all-to-all-done.1 = bf16[32,1,2,112,384]{4,3,2,1,0:T(8,128)(2,1)} async-done(((bf16[32,1,2,112,384]{4,3,2,1,0:T(8,128)(2,1)}), bf16[32,1,2,112,384]{4,3,2,1,0:T(8,128)(2,1)}, u32[]{:S(2)}, u32[]{:S(2)}) %all-to-all-start.1) | async-done | bytes 5505056 | tf_op jit(solution)/shard_map/all_to_all | solution.py:48
  169.3 4.0 gather_fusion.2
  173.3 1.9 fusion.36
  175.8 2.9 stack.32
  178.7 9.3 %all-to-all-start.2 = ((bf16[32,1,2,112,384]{4,3,2,1,0:T(8,128)(2,1)}), bf16[32,1,2,112,384]{4,3,2,1,0:T(8,128)(2,1)}, u32[]{:S(2)}, u32[]{:S(2)}) async-start(bf16[32,1,2,112,384]{4,3,2,1,0:T(8,128)(2,1)} %stack.32), calls=%async_computation.2 | async-start | bytes 11010048 | tf_op jit(solution)/shard_map/all_to_all | solution.py:48
  189.1 1.3 collective-permute-start.4
  190.4 1.3 collective-permute-start.5
  192.7 4.1 collective-permute-done.5
  197.8 2.4 convolution_bitcast_fusion
  200.2 52.3 %all-to-all-done.2 = bf16[32,1,2,112,384]{4,3,2,1,0:T(8,128)(2,1)} async-done(((bf16[32,1,2,112,384]{4,3,2,1,0:T(8,128)(2,1)}), bf16[32,1,2,112,384]{4,3,2,1,0:T(8,128)(2,1)}, u32[]{:S(2)}, u32[]{:S(2)}) %all-to-all-start.2) | async-done | bytes 5505056 | tf_op jit(solution)/shard_map/all_to_all | solution.py:48
  252.5 4.0 gather_fusion.3
  256.5 2.5 fusion.39
  259.1 1.8 copy.34
  262.0 1.9 convolution_bitcast_fusion.3
  265.2 1.3 dynamic-slice.2
  267.8 128.7 %all-reduce.4.cloned.1.call-done = f32[112,256]{0,1:T(8,128)} async-done(((f32[112,256]{0,1:T(8,128)}), f32[112,256]{0,1:T(8,128)}) %all-reduce.4.cloned.1.call-update) | async-done | bytes 114704
  397.2 31.3 %all-reduce.1 = bf16[112,8]{0,1:T(8,128)(2,1)S(1)} all-reduce(f32[112,8]{0,1:T(8,128)S(1)} %constant_dynamic-slice_fusion), channel_id=3, replica_groups=mesh['areal'=32,'layer'=16] {'layer'}, use_global_device_ids=true, to_apply=%region_3.4.clone | all-reduce | flops 896 | bytes 5376
  (35 shorter events, 14.3 us)
Async XLA Ops:
  7.2 83.0 %copy-start = (bf16[1,2,6,384,384]{4,3,2,1,0:T(8,128)(2,1)S(1)}, bf16[1,2,6,384,384]{4,3,2,1,0:T(8,128)(2,1)}, u32[]{:S(2)}) copy-start(bf16[1,2,6,384,384]{4,3,2,1,0:T(8,128)(2,1)} %param.11) | copy-start | bytes 10616836
  11.2 16.0 %copy-start.5 = (s32[1,1,6]{2,1,0:T(1,128)S(1)}, s32[1,1,6]{2,1,0:T(1,128)}, u32[]{:S(2)}) copy-start(s32[1,1,6]{2,1,0:T(1,128)} %param.13) | copy-start | bytes 76
  11.2 16.0 %copy-start.1 = (s32[64]{0:T(128)S(1)}, s32[64]{0:T(128)}, u32[]{:S(2)}) copy-start(s32[64]{0:T(128)} %param.15) | copy-start | bytes 772
  11.2 75.0 %all-to-all-start = ((bf16[32,1,2,112,384]{4,3,2,1,0:T(8,128)(2,1)}), bf16[32,1,2,112,384]{4,3,2,1,0:T(8,128)(2,1)}, u32[]{:S(2)}, u32[]{:S(2)}) async-start(bf16[32,1,2,112,384]{4,3,2,1,0:T(8,128)(2,1)} %stack.24), calls=%async_computation | async-start | bytes 11010048 | tf_op jit(solution)/shard_map/all_to_all | solution.py:48
  23.3 4.6 %collective-permute-start = (bf16[1,1,112,384]{3,2,1,0:T(8,128)(2,1)}, bf16[1,1,112,384]{3,2,1,0:T(8,128)(2,1)}, u32[]{:S(2)}, u32[]{:S(2)}) collective-permute-start(bf16[1,1,112,384]{3,2,1,0:T(8,128)(2,1)} %get-tuple-element.20), channel_id=1, source_target_pairs={{0,1},{1,2},{2,3},{3,4},{4,5},{5,6},{6,7},{7,8},{8,9},{9,10},{10,1... | collective-permute-start | bytes 258056 | tf_op jit(solution)/shard_map/ppermute | solution.py:16
  25.2 6.8 %collective-permute-start.1 = (bf16[1,1,112,384]{3,2,1,0:T(8,128)(2,1)}, bf16[1,1,112,384]{3,2,1,0:T(8,128)(2,1)}, u32[]{:S(2)}, u32[]{:S(2)}) collective-permute-start(bf16[1,1,112,384]{3,2,1,0:T(8,128)(2,1)} %get-tuple-element.21), channel_id=1, source_target_pairs={{1,0},{2,1},{3,2},{4,3},{5,4},{6,5},{7,6},{8,7},{9,8},{10,9},{11,1... | collective-permute-start | bytes 258056 | tf_op jit(solution)/shard_map/ppermute | solution.py:17
  92.0 0.7 copy-start.3
  95.6 73.6 %all-to-all-start.1 = ((bf16[32,1,2,112,384]{4,3,2,1,0:T(8,128)(2,1)}), bf16[32,1,2,112,384]{4,3,2,1,0:T(8,128)(2,1)}, u32[]{:S(2)}, u32[]{:S(2)}) async-start(bf16[32,1,2,112,384]{4,3,2,1,0:T(8,128)(2,1)} %stack.28), calls=%async_computation.1 | async-start | bytes 11010048 | tf_op jit(solution)/shard_map/all_to_all | solution.py:48
  105.7 3.7 collective-permute-start.2
  107.0 6.5 %collective-permute-start.3 = (bf16[1,1,112,384]{3,2,1,0:T(8,128)(2,1)S(1)}, bf16[1,1,112,384]{3,2,1,0:T(8,128)(2,1)S(1)}, u32[]{:S(2)}, u32[]{:S(2)}) collective-permute-start(bf16[1,1,112,384]{3,2,1,0:T(8,128)(2,1)S(1)} %get-tuple-element.17), channel_id=1, source_target_pairs={{1,0},{2,1},{3,2},{4,3},{5,4},{6,5},{7,6},{8,7},{9,8},{10,9},{11,1... | collective-permute-start | bytes 258056 | tf_op jit(solution)/shard_map/ppermute | solution.py:17
  175.1 0.7 copy-start.2
  178.7 9.3 %copy-start.4 = (f32[1,2,3,128]{3,1,2,0:T(2,128)S(1)}, f32[1,2,3,128]{3,1,2,0:T(2,128)}, u32[]{:S(2)}) copy-start(f32[1,2,3,128]{3,1,2,0:T(2,128)} %param.18) | copy-start | bytes 9220
  178.7 73.8 %all-to-all-start.2 = ((bf16[32,1,2,112,384]{4,3,2,1,0:T(8,128)(2,1)}), bf16[32,1,2,112,384]{4,3,2,1,0:T(8,128)(2,1)}, u32[]{:S(2)}, u32[]{:S(2)}) async-start(bf16[32,1,2,112,384]{4,3,2,1,0:T(8,128)(2,1)} %stack.32), calls=%async_computation.2 | async-start | bytes 11010048 | tf_op jit(solution)/shard_map/all_to_all | solution.py:48
  188.0 208.5 %all-reduce.4.cloned.1.call-start = ((), (), s32[]{:S(2)}) async-start(), calls=%async_computation.3 | async-start | bytes 262144
  189.1 3.7 collective-permute-start.4
  190.4 6.5 %collective-permute-start.5 = (bf16[1,1,112,384]{3,2,1,0:T(8,128)(2,1)S(1)}, bf16[1,1,112,384]{3,2,1,0:T(8,128)(2,1)S(1)}, u32[]{:S(2)}, u32[]{:S(2)}) collective-permute-start(bf16[1,1,112,384]{3,2,1,0:T(8,128)(2,1)S(1)} %get-tuple-element.13), channel_id=1, source_target_pairs={{1,0},{2,1},{3,2},{4,3},{5,4},{6,5},{7,6},{8,7},{9,8},{10,9},{11,1... | collective-permute-start | bytes 258056 | tf_op jit(solution)/shard_map/ppermute | solution.py:17
Sparse Core Ops, SparseCore 0:
  264.1 132.3 all-reduce.3
